TPU v7x, 32 devices: a whole 2x2x4 slice. The times are simulated.
32 devices in a mesh: dp: 2 (over x), expert: 16 (over z, y, core).
Axes of the slice: x: 2, y: 2, z: 4, core: 2. Of those that a mesh axis runs over, the one named last changes fastest.
Arguments:
- tokens: bfloat16 [1024, 7168], P('expert', 'dp'), may hold values from -6 to 6
- cotangent: bfloat16 [1024, 7168], P('expert', 'dp'), may hold values from -6 to 6
- expert_ids: int32 [1024, 8], P('expert'), may hold values from 0 to 15, all different within a row; in each aligned block of 64 rows (0 to 63, 64 to 127, ...) at most 40 rows name the same one
- gate_values: float32 [1024, 8], P('expert'), may hold values from 0.05 to 1
- gate_up_weight: bfloat16 [16, 2, 7168, 1024], P('expert', None, None, 'dp'), may hold values from -0.0625 to 0.0625
- down_weight: bfloat16 [16, 1024, 7168], P('expert', 'dp'), may hold values from -0.1875 to 0.1875
Outputs:
- output: bfloat16 [1024, 7168], P('expert', 'dp')
- input_grad: bfloat16 [1024, 7168], P('expert', 'dp')
- grad_gate_up: bfloat16 [16, 2, 7168, 1024], P('expert', None, None, 'dp')
- grad_down: bfloat16 [16, 1024, 7168], P('expert', 'dp')
Inputs may be any that keep to these rules, and one draw needn't show every extreme that they name: `expert_ids`: each row names 8 different experts. Within the rows of one device (aligned blocks of 64 rows) no expert is named by more than 40 rows, and in some block one expert is named by exactly 40 rows.
All inputs are finite; a program needn't handle non-finite values.
Results may differ from a plain program's by a relative error of at most 0.013.
Values may be sent and summed in bfloat16 or wider, within the bound.
A program may use at most 192 MiB of HBM per device.

v0:
```python
import jax
import jax.numpy as jnp
from jax import lax
from jax.sharding import PartitionSpec as P


def slot_tables(expert_ids, gate_values, expert_count, capacity):
    token_rows, top_count = expert_ids.shape
    flat_ids = expert_ids.reshape(-1)
    matches = (flat_ids[:, None] == jnp.arange(expert_count, dtype=jnp.int32)[None, :]).astype(
        jnp.int32
    )
    earlier = jnp.cumsum(matches, axis=0) - matches
    position = jnp.sum(earlier * matches, axis=1)
    target = flat_ids * capacity + position
    placed = (
        target[:, None] == jnp.arange(expert_count * capacity, dtype=jnp.int32)[None, :]
    ).astype(jnp.float32)
    placed = placed.reshape(token_rows, top_count, expert_count * capacity)
    scatter_table = jnp.sum(placed, axis=1)
    weight_table = jnp.sum(placed * gate_values[:, :, None], axis=1)
    return (scatter_table, weight_table)


def body(tokens, cotangent, expert_ids, gate_values, gate_up_weight, down_weight):
    expert_count = lax.axis_size("expert")
    token_rows = tokens.shape[0]
    top_count = expert_ids.shape[1]
    capacity = min(token_rows, 5 * token_rows * top_count // (4 * expert_count))
    model_width = gate_up_weight.shape[2]
    scatter_table, weight_table = slot_tables(expert_ids, gate_values, expert_count, capacity)
    dispatch_mat = scatter_table.T.astype(jnp.bfloat16)
    highest = lax.Precision.HIGHEST
    token_slots = jnp.dot(dispatch_mat, tokens, preferred_element_type=jnp.float32).astype(
        jnp.bfloat16
    )
    grad_slots = jnp.dot(weight_table.T, cotangent.astype(jnp.float32), precision=highest).astype(
        jnp.bfloat16
    )
    arrived = (
        lax.all_to_all(
            token_slots.reshape(expert_count, capacity, -1),
            "expert",
            split_axis=0,
            concat_axis=0,
            tiled=True,
        ),
        lax.all_to_all(
            grad_slots.reshape(expert_count, capacity, -1),
            "expert",
            split_axis=0,
            concat_axis=0,
            tiled=True,
        ),
    )
    expert_in, expert_grad = (
        lax.all_gather(arrived[0], "dp", axis=2, tiled=True),
        lax.all_gather(arrived[1], "dp", axis=2, tiled=True),
    )
    rows_in = expert_in.reshape(-1, model_width)
    grad_in = expert_grad.reshape(-1, model_width)
    gate_up_local = gate_up_weight[0]
    down_local = down_weight[0]
    pre = jnp.einsum("pd,cdh->pch", rows_in, gate_up_local, preferred_element_type=jnp.float32)
    gate_pre = pre[:, 0]
    up_pre = pre[:, 1]
    sigmoid_gate = jax.nn.sigmoid(gate_pre)
    silu_gate = gate_pre * sigmoid_gate
    hidden = (silu_gate * up_pre).astype(jnp.bfloat16)
    partial_out = jnp.dot(hidden, down_local, preferred_element_type=jnp.float32)
    grad_hidden = jnp.einsum("pd,hd->ph", grad_in, down_local, preferred_element_type=jnp.float32)
    grad_gate = (
        grad_hidden * up_pre * sigmoid_gate * (1.0 + gate_pre * (1.0 - sigmoid_gate))
    ).astype(jnp.bfloat16)
    grad_up = (grad_hidden * silu_gate).astype(jnp.bfloat16)
    grad_pre = jnp.stack([grad_gate, grad_up], axis=1)
    grad_down = jnp.einsum("ph,pd->hd", hidden, grad_in, preferred_element_type=jnp.float32).astype(
        jnp.bfloat16
    )[None]
    grad_gate_up = jnp.einsum(
        "pd,pch->cdh", rows_in, grad_pre, preferred_element_type=jnp.float32
    ).astype(jnp.bfloat16)[None]
    input_part = jnp.einsum(
        "pch,cdh->pd", grad_pre, gate_up_local, preferred_element_type=jnp.float32
    )
    summed_out, summed_in = (
        lax.psum_scatter(
            partial_out.astype(jnp.bfloat16), "dp", scatter_dimension=1, tiled=True
        ).astype(jnp.float32),
        lax.psum_scatter(
            input_part.astype(jnp.bfloat16), "dp", scatter_dimension=1, tiled=True
        ).astype(jnp.float32),
    )
    out_rows = summed_out.astype(jnp.bfloat16).reshape(expert_count, capacity, -1)
    in_rows = summed_in.astype(jnp.bfloat16).reshape(expert_count, capacity, -1)
    back_out, back_in = (
        lax.all_to_all(out_rows, "expert", split_axis=0, concat_axis=0, tiled=True),
        lax.all_to_all(in_rows, "expert", split_axis=0, concat_axis=0, tiled=True),
    )
    feature_width = back_out.shape[2]
    output = jnp.dot(
        weight_table, back_out.reshape(-1, feature_width).astype(jnp.float32), precision=highest
    ).astype(jnp.bfloat16)
    input_grad = jnp.dot(
        scatter_table, back_in.reshape(-1, feature_width).astype(jnp.float32), precision=highest
    ).astype(jnp.bfloat16)
    return (output, input_grad, grad_gate_up, grad_down)


def solution(mesh):
    return jax.shard_map(
        body,
        mesh=mesh,
        in_specs=(
            P("expert", "dp"),
            P("expert", "dp"),
            P("expert", None),
            P("expert", None),
            P("expert", None, None, "dp"),
            P("expert", "dp", None),
        ),
        out_specs=(
            P("expert", "dp"),
            P("expert", "dp"),
            P("expert", None, None, "dp"),
            P("expert", "dp", None),
        ),
        check_vma=False,
    )
```

profile of v0, /device:TPU:13, one launch (start us, length us, event | category | flops | bytes accessed | tf_op | source)
XLA Modules:
  0.0 723.0 jit_solution(5931990658518811433)
XLA Ops:
  7.2 0.0 copy-start
  7.2 0.0 all-gather.3.cloned.1.call-start
  7.2 0.8 copy.30
  8.0 0.1 eq.43
  8.1 0.1 eq.39
  8.2 1.2 reduce-window.6
  9.4 0.2 slice_reduce_fusion
  9.7 0.1 fusion.26
  9.8 0.1 reduce_sum.30
  9.8 0.1 copy.33
  9.9 0.7 multiply_add_fusion
  10.6 0.1 copy.34
  10.7 0.8 copy.35
  11.5 0.8 convert_reduce_fusion
  12.3 0.0 copy-done
  12.3 1.4 convolution_convert_fusion.3
  13.7 107.1 %all_to_all.20 = bf16[16,40,3584]{2,1,0:T(8,128)(2,1)} all-to-all(bf16[16,40,3584]{2,1,0:T(8,128)(2,1)S(1)} %bitcast.107), channel_id=1, replica_groups=mesh['dp'=2,'expert'=16] {'expert'}, dimensions={0} | all-to-all | bytes 9175040 | tf_op jit(solution)/shard_map/all_to_all | solution.py:41
  120.8 0.0 copy-start.4
  120.8 0.0 all-gather.3.cloned.1.call-update
  120.9 0.0 all-gather.5.cloned.1.call-start
  120.9 0.9 copy-done.4
  121.8 4.0 convolution_convert_fusion.2
  125.9 106.2 %all_to_all.21 = bf16[16,40,3584]{2,1,0:T(8,128)(2,1)} all-to-all(bf16[16,40,3584]{2,1,0:T(8,128)(2,1)S(1)} %bitcast.108), channel_id=1, replica_groups=mesh['dp'=2,'expert'=16] {'expert'}, dimensions={0} | all-to-all | bytes 9175040 | tf_op jit(solution)/shard_map/all_to_all | solution.py:48
  232.1 0.0 all-gather.5.cloned.1.call-update
  232.1 0.2 reduce-scatter.5.cloned.1.call-start
  232.3 3.7 all-gather.3.cloned.1.call-done
  236.0 14.3 %fusion.2 = f32[640,2,512]{2,0,1:T(8,128)S(1)} fusion(bf16[640,7168,1]{1,0,2:T(8,128)(2,1)} %bitcast.111, bf16[1,2,7168,512]{3,2,1,0:T(8,128)(2,1)} %param.10), kind=kOutput, calls=%fused_computation.3 | convolution fusion | flops 9395240960 | bytes 26476544 | tf_op jit(solution)/shard_map/pd,cdh->pch/dot_general | solution.py:64
  250.3 102.4 %all-gather.5.cloned.1.call-done = bf16[16,40,7168]{2,1,0:T(8,128)(2,1)} async-done(((bf16[16,40,3584]{2,1,0:T(8,128)(2,1)}), bf16[16,40,7168]{2,1,0:T(8,128)(2,1)}) %all-gather.5.cloned.1.call-update) | async-done | bytes 9175056 | tf_op jit(solution)/shard_map/all_gather | solution.py:58
  352.8 11.0 %fusion.22 = (bf16[640,1,512]{2,0,1:T(8,128)(2,1)S(1)}, bf16[640,1,512]{2,0,1:T(8,128)(2,1)S(1)}) fusion(f32[640,2,512]{2,0,1:T(8,128)S(1)} %fusion.2, bf16[640,7168]{1,0:T(8,128)(2,1)} %bitcast.113, bf16[1,512,7168]{2,1,0:T(8,128)(2,1)} %param.11), kind=kOutput, calls=%fused_computation.37 | convolution fusion | flops 4701880320 | bytes 20447232 | tf_op jit(solution)/shard_map/pd,hd->ph/dot_general | solution.py:71
  363.7 0.0 copy-start.5
  363.7 0.0 copy-start.7
  363.8 0.8 copy-done.5
  364.6 0.2 copy-done.7
  364.8 20.3 %bitcast_convert_fusion = bf16[640,7168]{1,0:T(8,128)(2,1)} fusion(bf16[1,2,7168,512]{3,2,1,0:T(8,128)(2,1)} %param.10, bf16[640,1,512]{2,0,1:T(8,128)(2,1)S(1)} %get-tuple-element.23, bf16[640,1,512]{2,0,1:T(8,128)(2,1)S(1)} %get-tuple-element.22), kind=kOutput, calls=%fused_computation | convolution fusion | flops 9400483840 | bytes 25165824 | tf_op jit(solution)/shard_map/pch,cdh->pd/dot_general | solution.py:83
  385.1 0.0 reduce-scatter.5.cloned.1.call-update
  385.1 0.3 reduce-scatter.3.cloned.1.call-start
  385.4 0.4 multiply_convert_fusion
  385.8 0.0 copy-start.2
  385.8 0.8 copy-done.2
  386.6 10.3 %convolution_convert_fusion = bf16[640,7168]{1,0:T(8,128)(2,1)} fusion(bf16[1,512,7168]{2,1,0:T(8,128)(2,1)} %param.11, bf16[640,1,512]{2,0,1:T(8,128)(2,1)S(1)} %multiply_convert_fusion), kind=kOutput, calls=%fused_computation.6 | convolution fusion | flops 4702208000 | bytes 17170432 | tf_op jit(solution)/shard_map/dot_general | solution.py:70
  397.0 0.0 reduce-scatter.3.cloned.1.call-update
  397.0 96.0 %reduce-scatter.5.cloned.1.call-done = bf16[640,3584]{1,0:T(8,128)(2,1)} async-done(((bf16[640,7168]{1,0:T(8,128)(2,1)}), bf16[640,3584]{1,0:T(8,128)(2,1)}) %reduce-scatter.5.cloned.1.call-update) | async-done | bytes 4587536 | tf_op jit(solution)/shard_map/reduce_scatter | solution.py:90
  493.0 6.4 all-to-all-start.3
  499.4 104.1 %reduce-scatter.3.cloned.1.call-done = bf16[640,3584]{1,0:T(8,128)(2,1)} async-done(((bf16[640,7168]{1,0:T(8,128)(2,1)}), bf16[640,3584]{1,0:T(8,128)(2,1)}) %reduce-scatter.3.cloned.1.call-update) | async-done | bytes 4587536 | tf_op jit(solution)/shard_map/reduce_scatter | solution.py:87
  603.5 0.0 all-to-all-done.3
  603.5 0.0 copy-start.6
  603.5 0.0 copy-start.8
  603.5 6.5 all-to-all-start.1
  610.0 0.0 copy-done.6
  610.1 0.0 copy-done.8
  610.1 17.8 %convert_bitcast_fusion = bf16[1,2,7168,512]{2,3,1,0:T(8,128)(2,1)} fusion(bf16[640,7168,1]{1,0,2:T(8,128)(2,1)} %bitcast.112, bf16[640,1,512]{2,0,1:T(8,128)(2,1)S(1)} %copy-done.8, bf16[640,1,512]{2,0,1:T(8,128)(2,1)S(1)} %copy-done.6), kind=kOutput, calls=%fused_computation.5 | convolution fusion | flops 9403236352 | bytes 25165824 | tf_op jit(solution)/shard_map/pd,pch->cdh/dot_general | solution.py:80
  627.8 0.0 copy-start.3
  627.8 20.0 %copy.37 = bf16[1,2,7168,512]{3,2,1,0:T(8,128)(2,1)} copy(bf16[1,2,7168,512]{2,3,1,0:T(8,128)(2,1)} %convert_bitcast_fusion) | data formatting | bytes 29360128
  647.9 0.0 copy-done.3
  647.9 11.6 %fusion.6 = bf16[1,512,7168]{2,1,0:T(8,128)(2,1)} fusion(bf16[640,7168]{1,0:T(8,128)(2,1)} %bitcast.114, bf16[640,1,512]{2,0,1:T(8,128)(2,1)S(1)} %copy-done.3), kind=kOutput, calls=%fused_computation.8 | convolution fusion | flops 4701290496 | bytes 17170432 | tf_op jit(solution)/shard_map/ph,pd->hd/dot_general | solution.py:77
  659.4 0.0 copy-start.1
  659.4 5.6 convolution_convert_fusion.4
  665.0 45.9 %all-to-all-done.1 = bf16[16,40,3584]{2,1,0:T(8,128)(2,1)} async-done(((bf16[16,40,3584]{2,1,0:T(8,128)(2,1)}), bf16[16,40,3584]{2,1,0:T(8,128)(2,1)}, u32[]{:S(2)}, u32[]{:S(2)}) %all-to-all-start.1) | async-done | bytes 4587552 | tf_op jit(solution)/shard_map/all_to_all | solution.py:97
  710.9 5.5 convolution_convert_fusion.5
  716.5 0.0 copy-done.1
  (3 shorter events, 0.0 us)
Async XLA Ops:
  7.2 5.1 copy-start
  7.2 228.9 %all-gather.3.cloned.1.call-start = ((), (), s32[]{:S(2)}) async-start(), calls=%async_computation.6 | async-start | bytes 13762560 | tf_op jit(solution)/shard_map/all_gather | solution.py:57
  120.8 1.0 copy-start.4
  120.9 231.9 %all-gather.5.cloned.1.call-start = ((), (), s32[]{:S(2)}) async-start(), calls=%async_computation.8 | async-start | bytes 13762560 | tf_op jit(solution)/shard_map/all_gather | solution.py:58
  232.1 260.9 %reduce-scatter.5.cloned.1.call-start = ((), (), s32[]{:S(2)}) async-start(), calls=%async_computation.9 | async-start | bytes 13762560 | tf_op jit(solution)/shard_map/reduce_scatter | solution.py:90
  363.7 0.9 copy-start.5
  363.7 1.0 copy-start.7
  385.1 218.4 %reduce-scatter.3.cloned.1.call-start = ((), (), s32[]{:S(2)}) async-start(), calls=%async_computation.7 | async-start | bytes 13762560 | tf_op jit(solution)/shard_map/reduce_scatter | solution.py:87
  385.8 0.8 copy-start.2
  493.0 110.5 %all-to-all-start.3 = ((bf16[16,40,3584]{2,1,0:T(8,128)(2,1)}), bf16[16,40,3584]{2,1,0:T(8,128)(2,1)}, u32[]{:S(2)}, u32[]{:S(2)}) async-start(bf16[16,40,3584]{2,1,0:T(8,128)(2,1)} %bitcast.110), calls=%async_computation.5 | async-start | bytes 9175040 | tf_op jit(solution)/shard_map/all_to_all | solution.py:98
  603.5 6.5 copy-start.6
  603.5 6.5 copy-start.8
  603.5 107.4 %all-to-all-start.1 = ((bf16[16,40,3584]{2,1,0:T(8,128)(2,1)}), bf16[16,40,3584]{2,1,0:T(8,128)(2,1)}, u32[]{:S(2)}, u32[]{:S(2)}) async-start(bf16[16,40,3584]{2,1,0:T(8,128)(2,1)} %bitcast.109), calls=%async_computation.2 | async-start | bytes 9175040 | tf_op jit(solution)/shard_map/all_to_all | solution.py:97
  627.8 20.0 %copy-start.3 = (bf16[640,1,512]{2,0,1:T(8,128)(2,1)S(1)}, bf16[640,1,512]{2,0,1:T(8,128)(2,1)}, u32[]{:S(2)}) copy-start(bf16[640,1,512]{2,0,1:T(8,128)(2,1)} %copy-done.2) | copy-start | bytes 1966084
  659.4 57.0 %copy-start.1 = (bf16[64,3584]{1,0:T(8,128)(2,1)S(1)}, bf16[64,3584]{1,0:T(8,128)(2,1)}, u32[]{:S(2)}) copy-start(bf16[64,3584]{1,0:T(8,128)(2,1)} %param.6) | copy-start | bytes 1376260
Sparse Core Ops, SparseCore 0:
  121.0 115.0 all-gather.2
  237.6 115.1 all-gather.4
  385.3 107.7 reduce-scatter.4
  495.8 107.6 reduce-scatter.2
where the time goes:
time: 724 us; the launch traced here: 723 us
  waiting for transfers between devices  352 us (49%)
  blocking collectives  213 us (29%)
  matrix products  102 us (14%)
  local copies, waits for them, and re-layouts  25.1 us (3%)
  between operations  13.9 us (2%)
  starting transfers between devices  13.5 us (2%)
    all_to_all x1, blocking collectives, body(): lax.all_to_all(token_slots.reshape(expert_count, capacity, -1), 'expert',...  107 us
    all_to_all x1, blocking collectives, body(): lax.all_to_all(grad_slots.reshape(expert_count, capacity, -1), 'expert',...  106 us
    reduce_scatter x1, waiting for transfers between devices, body(): lax.psum_scatter(partial_out.astype(jnp.bfloat16), 'dp', scatter_dimensio...  104 us
    all_gather x1, waiting for transfers between devices, body(): lax.all_gather(arrived[1], 'dp', axis=2, tiled=True)  102 us
    reduce_scatter x1, waiting for transfers between devices, body(): lax.psum_scatter(input_part.astype(jnp.bfloat16), 'dp', scatter_dimension...  96 us
    all_to_all x1, waiting for transfers between devices, body(): lax.all_to_all(out_rows, 'expert', split_axis=0, concat_axis=0, tiled=True)  45.9 us
    unnamed x21, local copies, waits for them, and re-layouts  24.4 us
    dot_general x1, matrix products, body(): jnp.einsum('pch,cdh->pd', grad_pre, gate_up_local, preferred_element_type...  20.3 us
  transfers between devices with their start and end apart: 6, of which 5 were waited for; matrix products, arithmetic and copies ran while one was open for 12% of the time, Pallas kernels for 0%

commit v1 on v0

v1 whole, which is shorter than its diff:
```python
import jax
import jax.numpy as jnp
from jax import lax
from jax.sharding import PartitionSpec as P


def expert_gates(expert_ids, gate_values, expert_count):
    named = expert_ids[:, :, None] == jnp.arange(expert_count, dtype=jnp.int32)
    return jnp.sum(jnp.where(named, gate_values[:, :, None], 0.0), axis=1)


def body(tokens, cotangent, expert_ids, gate_values, gate_up_weight, down_weight):
    expert_count = lax.axis_size("expert")
    parts = lax.axis_size("dp")
    rows, width = tokens.shape
    both = ("dp", "expert")
    f32 = jnp.float32
    bf16 = jnp.bfloat16
    gates = lax.all_gather(
        expert_gates(expert_ids, gate_values, expert_count), "expert", axis=0, tiled=True
    )
    gate = lax.dynamic_slice_in_dim(gates, lax.axis_index("expert"), 1, axis=1)
    gate_weight = gate_up_weight[0, 0]
    up_weight = gate_up_weight[0, 1]
    down = down_weight[0]
    spans = [slice(p * width, (p + 1) * width) for p in range(parts)]
    cols = (((1,), (1,)), ((), ()))
    over = (((0,), (0,)), ((), ()))

    def dot(x, y, dims=(((1,), (0,)), ((), ()))):
        return lax.dot_general(x, y, dims, preferred_element_type=f32)

    def gathered(x):
        return lax.all_gather(x, both, axis=0, tiled=False).reshape(parts, -1, width)

    def scattered(pieces):
        x = jnp.concatenate(pieces, axis=0).reshape(parts * expert_count, rows, width)
        return lax.psum_scatter(x, both, scatter_dimension=0, tiled=False)

    x = gathered(tokens)
    c = gathered(cotangent)
    a = sum(dot(x[p], gate_weight[spans[p]]) for p in range(parts))
    b = sum(dot(x[p], up_weight[spans[p]]) for p in range(parts))
    s = jax.nn.sigmoid(a)
    silu = a * s
    hidden = (silu * b).astype(bf16)
    output = scattered([(dot(hidden, down[:, span]) * gate).astype(bf16) for span in spans])
    back = [(c[p].astype(f32) * gate).astype(bf16) for p in range(parts)]
    grad_hidden = sum(dot(back[p], down[:, spans[p]], cols) for p in range(parts))
    grad_gate = (grad_hidden * b * s * (1.0 + a * (1.0 - s))).astype(bf16)
    grad_up = (grad_hidden * silu).astype(bf16)
    input_grad = scattered(
        [
            (
                dot(grad_gate, gate_weight[span], cols) + dot(grad_up, up_weight[span], cols)
            ).astype(bf16)
            for span in spans
        ]
    )
    grad_down = jnp.concatenate([dot(hidden, k, over).astype(bf16) for k in back], axis=1)
    grad_gate_up = jnp.stack(
        [
            jnp.concatenate([dot(x[p], g, over).astype(bf16) for p in range(parts)], axis=0)
            for g in (grad_gate, grad_up)
        ]
    )
    return (output, input_grad, grad_gate_up[None], grad_down[None])


def solution(mesh):
    return jax.shard_map(
        body,
        mesh=mesh,
        in_specs=(
            P("expert", "dp"),
            P("expert", "dp"),
            P("expert", None),
            P("expert", None),
            P("expert", None, None, "dp"),
            P("expert", "dp", None),
        ),
        out_specs=(
            P("expert", "dp"),
            P("expert", "dp"),
            P("expert", None, None, "dp"),
            P("expert", "dp", None),
        ),
        check_vma=False,
    )
```

time: 724 us -> 603 us (0.83)
  blocking collectives: 213 us -> 16 us
  matrix products: 102 us -> 152 us
  other arithmetic: 3.21 us -> 48.8 us
  starting transfers between devices: 13.5 us -> 0.16 us
  waiting for transfers between devices: 352 us -> 344 us
    all_to_all x2 -> x0, blocking collectives: 213 us -> none  [the longest x1 107 us: body(): lax.all_to_all(token_slots.reshape(expert_count, capacity, -1), 'expert',...]
    all_gather x2, waiting for transfers between devices: 106 us -> 167 us  [gathered(): lax.all_gather(x, both, axis=0, tiled=False).reshape(parts, -1, width)]
    dot_general x10 -> x18, matrix products: 102 us -> 152 us  [dot(): return lax.dot_general(x, y, dims, preferred_element_type=f32)]
    all_to_all x2 -> x0, waiting for transfers between devices: 45.9 us -> none  [the longest x1 45.9 us: body(): lax.all_to_all(out_rows, 'expert', split_axis=0, concat_axis=0, tiled=True)]
    reduce_scatter x2, waiting for transfers between devices: 200 us -> 176 us  [scattered(): return lax.psum_scatter(x, both, scatter_dimension=0, tiled=False)]
    broadcast_in_dim x0 -> x2, other arithmetic: none -> 19.4 us  [body(): return (output, input_grad, grad_gate_up[None], grad_down[None])]
    all_gather x0 -> x1, blocking collectives: none -> 16 us  [body(): lax.all_gather(expert_gates(expert_ids, gate_values, expert_count), 'expe...]
    concatenate x0 -> x2, other arithmetic: none -> 15.5 us  [scattered(): jnp.concatenate(pieces, axis=0).reshape(parts * expert_count, rows, width)]
  transfers between devices with their start and end apart: 6 -> 4, of which waited for: 5 -> 4; matrix products, arithmetic and copies ran while one was open for 12% -> 31% of each run, Pallas kernels for 0% -> 0%
where the time goes in v1:
time: 603 us; the launch traced here: 596 us
  waiting for transfers between devices  344 us (57%)
  matrix products  152 us (25%)
  other arithmetic  48.8 us (8%)
  local copies, waits for them, and re-layouts  20.4 us (3%)
  blocking collectives  16 us (3%)
  between operations  14.2 us (2%)
    reduce_scatter x2, waiting for transfers between devices, scattered(): return lax.psum_scatter(x, both, scatter_dimension=0, tiled=False)  176 us
    all_gather x2, waiting for transfers between devices, gathered(): lax.all_gather(x, both, axis=0, tiled=False).reshape(parts, -1, width)  167 us
    dot_general x18, matrix products, dot(): return lax.dot_general(x, y, dims, preferred_element_type=f32)  152 us
    unnamed x32, local copies, waits for them, and re-layouts  20.4 us
    broadcast_in_dim x2, other arithmetic, body(): return (output, input_grad, grad_gate_up[None], grad_down[None])  19.4 us
    all_gather x1, blocking collectives, body(): lax.all_gather(expert_gates(expert_ids, gate_values, expert_count), 'expe...  16 us
    concatenate x2, other arithmetic, scattered(): jnp.concatenate(pieces, axis=0).reshape(parts * expert_count, rows, width)  15.5 us
    another operation x2, other arithmetic, body(): jnp.stack([jnp.concatenate([dot(x[p], g, over).astype(bf16) for p in rang...  13.1 us
  transfers between devices with their start and end apart: 4, of which 4 were waited for; matrix products, arithmetic and copies ran while one was open for 31% of the time, Pallas kernels for 0%

profile of v1, /device:TPU:13, one launch (start us, length us, event | category | flops | bytes accessed | tf_op | source)
XLA Modules:
  0.0 595.8 jit_solution(7872292042143336398)
XLA Ops:
  7.2 0.0 all-gather.6.cloned.1.call-start
  7.2 0.7 all-gather.6.cloned.1.call-update
  7.9 0.0 all-gather.8.cloned.1.call-start
  7.9 0.7 all-gather.8.cloned.1.call-update
  8.6 0.0 reduce-scatter.3.cloned.1.call-start
  8.7 0.7 select_reduce_fusion
  9.4 16.0 %all-gather.2 = f32[16,64,16]{1,2,0:T(8,128)S(1)} all-gather(f32[1,64,16]{1,2,0:T(8,128)S(1)} %bitcast.63), channel_id=1, replica_groups=mesh['dp'=2,'expert'=16] {'expert'}, dimensions={0}, use_global_device_ids=true | all-gather | bytes 69632 | tf_op jit(solution)/shard_map/all_gather | solution.py:19
  25.5 0.1 reshape.51
  25.6 91.6 %all-gather.6.cloned.1.call-done = bf16[2048,3584]{1,0:T(8,128)(2,1)} async-done(((bf16[64,3584]{1,0:T(8,128)(2,1)}), bf16[2048,3584]{1,0:T(8,128)(2,1)}) %all-gather.6.cloned.1.call-update) | async-done | bytes 14680080 | tf_op jit(solution)/shard_map/all_gather | solution.py:34
  117.2 0.0 copy-start.1
  117.2 0.0 slice-start
  117.2 9.5 %fusion.9 = f32[1024,512]{1,0:T(8,128)} fusion(bf16[2048,3584]{1,0:T(8,128)(2,1)} %all-gather.6.cloned.1.call-done, bf16[1,2,7168,512]{3,2,1,0:T(8,128)(2,1)} %param.10), kind=kOutput, calls=%fused_computation.27 | convolution fusion | flops 3758096384 | bytes 13107200 | tf_op jit(solution)/shard_map/dot_general | solution.py:31
  126.7 0.0 copy-done.1
  126.7 8.5 %fusion.7 = f32[1024,512]{1,0:T(8,128)} fusion(bf16[2048,3584]{1,0:T(8,128)(2,1)S(1)} %copy-done.1, bf16[1,2,7168,512]{3,2,1,0:T(8,128)(2,1)} %param.10), kind=kOutput, calls=%fused_computation.25 | convolution fusion | flops 3758096384 | bytes 13107200 | tf_op jit(solution)/shard_map/dot_general | solution.py:31
  135.2 0.0 slice-done
  135.2 0.0 slice-done.1
  135.2 0.0 slice-done.2
  135.2 0.0 slice-done.3
  135.2 6.9 %fusion.52 = f32[1024,512]{1,0:T(8,128)} fusion(f32[1024,512]{1,0:T(8,128)} %fusion.9, bf16[1,2,7168,512]{3,2,1,0:T(8,128)(2,1)S(1)} %bitcast.71, bf16[2048,3584]{1,0:T(8,128)(2,1)S(1)} %copy-done.1), kind=kOutput, calls=%fused_computation.66 | convolution fusion | flops 3758620672 | bytes 15204352 | tf_op jit(solution)/shard_map/dot_general | solution.py:31
  142.1 6.3 %fusion.57 = f32[1024,512]{1,0:T(8,128)} fusion(f32[1024,512]{1,0:T(8,128)} %fusion.7, bf16[1,2,7168,512]{3,2,1,0:T(8,128)(2,1)S(1)} %bitcast.71, bf16[2048,3584]{1,0:T(8,128)(2,1)S(1)} %copy-done.1), kind=kOutput, calls=%fused_computation.67 | convolution fusion | flops 3758620672 | bytes 15204352 | tf_op jit(solution)/shard_map/dot_general | solution.py:31
  148.4 75.1 %all-gather.8.cloned.1.call-done = bf16[2048,3584]{1,0:T(8,128)(2,1)} async-done(((bf16[64,3584]{1,0:T(8,128)(2,1)}), bf16[2048,3584]{1,0:T(8,128)(2,1)}) %all-gather.8.cloned.1.call-update) | async-done | bytes 14680080 | tf_op jit(solution)/shard_map/all_gather | solution.py:34
  223.6 9.6 %fusion.28 = f32[1024,512]{1,0:T(8,128)} fusion(bf16[512,7168]{1,0:T(8,128)(2,1)} %bitcast.74, bf16[2048,3584]{1,0:T(8,128)(2,1)} %all-gather.8.cloned.1.call-done, f32[1024]{0:T(1024)S(1)} %bitcast.64), kind=kOutput, calls=%fused_computation.46 | convolution fusion | flops 3769106432 | bytes 13111296 | tf_op jit(solution)/shard_map/dot_general | solution.py:31
  233.2 0.0 copy-done
  233.2 9.6 %multiply_convert_fusion.2 = (bf16[1024,512]{1,0:T(8,128)(2,1)}, bf16[1024,512]{1,0:T(8,128)(2,1)S(1)}, bf16[1024,512]{1,0:T(8,128)(2,1)S(1)}) fusion(f32[1024,512]{1,0:T(8,128)} %fusion.52, f32[1024,512]{1,0:T(8,128)} %fusion.57, f32[1024,512]{1,0:T(8,128)} %fusion.28, bf16[512,7168]{1,0:T(8,128)(2,1)} %bitcast.75, bf16[2048,3584]{1,0:T(8,128)(2,1)S(1)} %copy-done, ...), kind=kOutput, calls=%fused_computation.60 | convolution fusion | flops 3777495040 | bytes 20451328 | tf_op jit(solution)/shard_map/dot_general | solution.py:31
  242.7 7.0 %multiply_convert_fusion = bf16[1024,3584]{1,0:T(8,128)(2,1)S(1)} fusion(bf16[1024,512]{1,0:T(8,128)(2,1)S(1)} %get-tuple-element.26, f32[1024]{0:T(1024)S(1)} %bitcast.66, bf16[512,7168]{1,0:T(8,128)(2,1)} %bitcast.76), kind=kOutput, calls=%fused_computation.9 | convolution fusion | flops 3765436416 | bytes 12062720 | tf_op jit(solution)/shard_map/dot_general | solution.py:31
  249.7 0.0 copy-done.5
  249.7 6.2 %multiply_convert_fusion.1 = bf16[1024,3584]{1,0:T(8,128)(2,1)S(1)} fusion(bf16[1024,512]{1,0:T(8,128)(2,1)S(1)} %get-tuple-element.26, f32[1024]{0:T(1024)S(1)} %bitcast.67, bf16[512,7168]{1,0:T(8,128)(2,1)} %bitcast.77), kind=kOutput, calls=%fused_computation.10 | convolution fusion | flops 3765436416 | bytes 12062720 | tf_op jit(solution)/shard_map/dot_general | solution.py:31
  256.0 6.0 %pad_maximum_fusion = bf16[2048,3584]{1,0:T(8,128)(2,1)} fusion(bf16[1024,3584]{1,0:T(8,128)(2,1)S(1)} %multiply_convert_fusion, bf16[1024,3584]{1,0:T(8,128)(2,1)S(1)} %multiply_convert_fusion.1), kind=kLoop, calls=%fused_computation | loop fusion | flops 29360128 | bytes 29360128 | tf_op jit(solution)/shard_map/concatenate | solution.py:37
  262.0 0.0 reduce-scatter.3.cloned.1.call-update
  262.0 0.0 reduce-scatter.5.cloned.1.call-start
  262.1 9.8 %fusion.22 = f32[1024,3584]{1,0:T(8,128)} fusion(bf16[1024,512]{1,0:T(8,128)(2,1)S(1)} %get-tuple-element.25, bf16[1,2,7168,512]{3,2,1,0:T(8,128)(2,1)} %param.10), kind=kOutput, calls=%fused_computation.40 | convolution fusion | flops 3758096384 | bytes 19398656 | tf_op jit(solution)/shard_map/dot_general | solution.py:31
  271.9 0.0 copy-done.2
  271.9 9.5 %fusion.25 = f32[1024,3584]{1,0:T(8,128)} fusion(bf16[1024,512]{1,0:T(8,128)(2,1)S(1)} %get-tuple-element.25, bf16[1,2,7168,512]{3,2,1,0:T(8,128)(2,1)} %param.10), kind=kOutput, calls=%fused_computation.43 | convolution fusion | flops 3758096384 | bytes 19398656 | tf_op jit(solution)/shard_map/dot_general | solution.py:31
  281.3 10.8 %add_convert_fusion = bf16[1024,3584]{1,0:T(8,128)(2,1)S(1)} fusion(f32[1024,3584]{1,0:T(8,128)} %fusion.22, bf16[1024,512]{1,0:T(8,128)(2,1)} %get-tuple-element.24, bf16[1,2,7168,512]{3,2,1,0:T(8,128)(2,1)} %param.10), kind=kOutput, calls=%fused_computation.7 | convolution fusion | flops 3765436416 | bytes 26738688 | tf_op jit(solution)/shard_map/dot_general | solution.py:31
  292.1 13.9 %add_convert_fusion.1 = bf16[1024,3584]{1,0:T(8,128)(2,1)} fusion(f32[1024,3584]{1,0:T(8,128)} %fusion.25, bf16[1024,512]{1,0:T(8,128)(2,1)} %get-tuple-element.24, bf16[1,2,7168,512]{3,2,1,0:T(8,128)(2,1)} %param.10), kind=kOutput, calls=%fused_computation.8 | convolution fusion | flops 3765436416 | bytes 26738688 | tf_op jit(solution)/shard_map/dot_general | solution.py:31
  306.0 9.5 %pad_maximum_fusion.1 = bf16[2048,3584]{1,0:T(8,128)(2,1)} fusion(bf16[1024,3584]{1,0:T(8,128)(2,1)S(1)} %add_convert_fusion, bf16[1024,3584]{1,0:T(8,128)(2,1)} %add_convert_fusion.1), kind=kLoop, calls=%fused_computation.1 | loop fusion | flops 29360128 | bytes 29360128 | tf_op jit(solution)/shard_map/concatenate | solution.py:37
  315.5 0.0 reduce-scatter.5.cloned.1.call-update
  315.5 0.0 copy-start.4
  315.5 0.0 slice-start.4
  315.5 0.0 slice-start.5
  315.5 7.6 %fusion.5 = bf16[3584,512]{0,1:T(8,128)(2,1)S(1)} fusion(bf16[1024,512]{1,0:T(8,128)(2,1)} %get-tuple-element.24, bf16[2048,3584]{1,0:T(8,128)(2,1)} %all-gather.6.cloned.1.call-done), kind=kOutput, calls=%fused_computation.23 | convolution fusion | flops 3759931392 | bytes 12058624 | tf_op jit(solution)/shard_map/dot_general | solution.py:31
  323.2 0.0 copy-done.4
  323.2 0.0 slice-start.6
  323.2 0.0 slice-start.7
  323.2 0.0 copy-start.3
  323.2 8.8 %fusion.4 = bf16[3584,512]{0,1:T(8,128)(2,1)} fusion(bf16[1024,512]{1,0:T(8,128)(2,1)S(1)} %copy-done.4, bf16[2048,3584]{1,0:T(8,128)(2,1)} %all-gather.6.cloned.1.call-done), kind=kOutput, calls=%fused_computation.22 | convolution fusion | flops 3759931392 | bytes 12058624 | tf_op jit(solution)/shard_map/dot_general | solution.py:31
  332.0 0.0 slice-done.4
  332.0 0.0 slice-done.5
  332.0 0.0 slice-done.6
  332.0 0.0 slice-done.7
  332.0 0.0 copy-done.3
  332.0 5.7 fusion.3
  337.7 5.6 fusion.2
  343.3 6.1 %maximum_bitcast_fusion.2 = bf16[1,7168,512]{1,2,0:T(8,128)(2,1)} fusion(bf16[3584,512]{0,1:T(8,128)(2,1)S(1)} %fusion.5, bf16[3584,512]{0,1:T(8,128)(2,1)} %fusion.4), kind=kLoop, calls=%fused_computation.12 | loop fusion | flops 14680064 | bytes 14680064 | tf_op jit(solution)/shard_map/stack | solution.py:61
  349.4 7.0 %maximum_bitcast_fusion.1 = bf16[1,7168,512]{1,2,0:T(8,128)(2,1)} fusion(bf16[3584,512]{0,1:T(8,128)(2,1)} %fusion.3, bf16[3584,512]{0,1:T(8,128)(2,1)} %fusion.2), kind=kLoop, calls=%fused_computation.11 | loop fusion | flops 14680064 | bytes 14680064 | tf_op jit(solution)/shard_map/stack | solution.py:61
  356.5 13.3 %maximum_bitcast_fusion = bf16[1,2,7168,512]{2,3,1,0:T(8,128)(2,1)} fusion(bf16[1,7168,512]{1,2,0:T(8,128)(2,1)} %maximum_bitcast_fusion.2, bf16[1,7168,512]{1,2,0:T(8,128)(2,1)} %maximum_bitcast_fusion.1), kind=kLoop, calls=%fused_computation.2 | loop fusion | flops 7340032 | bytes 29360128 | tf_op jit(solution)/shard_map/broadcast_in_dim | solution.py:67
  369.7 20.2 %copy.24 = bf16[1,2,7168,512]{3,2,1,0:T(8,128)(2,1)} copy(bf16[1,2,7168,512]{2,3,1,0:T(8,128)(2,1)} %maximum_bitcast_fusion) | data formatting | bytes 29360128
  390.0 0.0 copy-start.6
  390.0 8.0 %convolution_convert_fusion = bf16[512,3584]{1,0:T(8,128)(2,1)S(1)} fusion(bf16[1024,512]{1,0:T(8,128)(2,1)} %copy-done.5, bf16[2048,3584]{1,0:T(8,128)(2,1)} %all-gather.8.cloned.1.call-done, f32[1024]{0:T(1024)S(1)} %bitcast.68), kind=kOutput, calls=%fused_computation.14 | convolution fusion | flops 3770941440 | bytes 12062720 | tf_op jit(solution)/shard_map/dot_general | solution.py:31
  398.0 0.0 copy-done.6
  398.0 9.3 %convolution_convert_fusion.1 = bf16[512,3584]{1,0:T(8,128)(2,1)} fusion(bf16[1024,512]{1,0:T(8,128)(2,1)S(1)} %copy-done.6, bf16[2048,3584]{1,0:T(8,128)(2,1)} %all-gather.8.cloned.1.call-done, f32[1024]{0:T(1024)S(1)} %bitcast.69), kind=kOutput, calls=%fused_computation.15 | convolution fusion | flops 3770941440 | bytes 12062720 | tf_op jit(solution)/shard_map/dot_general | solution.py:31
  407.3 6.1 %maximum_bitcast_fusion.3 = bf16[1,512,7168]{2,1,0:T(8,128)(2,1)} fusion(bf16[512,3584]{1,0:T(8,128)(2,1)S(1)} %convolution_convert_fusion, bf16[512,3584]{1,0:T(8,128)(2,1)} %convolution_convert_fusion.1), kind=kLoop, calls=%fused_computation.13 | loop fusion | flops 14680064 | bytes 14680064 | tf_op jit(solution)/shard_map/broadcast_in_dim | solution.py:67
  413.4 8.8 %reduce-scatter.3.cloned.1.call-done = bf16[1,64,3584]{2,1,0:T(8,128)(2,1)} async-done(((bf16[32,64,3584]{2,1,0:T(8,128)(2,1)}), bf16[1,64,3584]{2,1,0:T(8,128)(2,1)}) %reduce-scatter.3.cloned.1.call-update) | async-done | bytes 458768 | tf_op jit(solution)/shard_map/reduce_scatter | solution.py:38
  422.2 166.8 %reduce-scatter.5.cloned.1.call-done = bf16[1,64,3584]{2,1,0:T(8,128)(2,1)} async-done(((bf16[32,64,3584]{2,1,0:T(8,128)(2,1)}), bf16[1,64,3584]{2,1,0:T(8,128)(2,1)}) %reduce-scatter.5.cloned.1.call-update) | async-done | bytes 458768 | tf_op jit(solution)/shard_map/reduce_scatter | solution.py:38
  (10 shorter events, 0.1 us)
Async XLA Ops:
  7.2 110.0 %all-gather.6.cloned.1.call-start = ((), (), s32[]{:S(2)}) async-start(), calls=%async_computation.4 | async-start | bytes 15138816 | tf_op jit(solution)/shard_map/all_gather | solution.py:34
  7.9 215.7 %all-gather.8.cloned.1.call-start = ((), (), s32[]{:S(2)}) async-start(), calls=%async_computation.5 | async-start | bytes 15138816 | tf_op jit(solution)/shard_map/all_gather | solution.py:34
  8.6 413.5 %reduce-scatter.3.cloned.1.call-start = ((), (), s32[]{:S(2)}) async-start(), calls=%async_computation.2 | async-start | bytes 15138816 | tf_op jit(solution)/shard_map/reduce_scatter | solution.py:38
  117.2 9.5 %copy-start.1 = (bf16[2048,3584]{1,0:T(8,128)(2,1)S(1)}, bf16[2048,3584]{1,0:T(8,128)(2,1)}, u32[]{:S(2)}) copy-start(bf16[2048,3584]{1,0:T(8,128)(2,1)} %all-gather.6.cloned.1.call-done) | copy-start | bytes 44040196
  117.2 18.1 %slice-start = ((s8[14680064]{0:T(1024)(128)(4,1)}), s8[4194304]{0:T(1024)(128)(4,1)S(1)}, s32[]{:S(2)}) async-start(s8[14680064]{0:T(1024)(128)(4,1)} %bitcast.70), calls=%async_computation.6 | async-start | bytes 8388608
  117.2 18.1 %slice-start.1 = ((s8[14680064]{0:T(1024)(128)(4,1)}), s8[4194304]{0:T(1024)(128)(4,1)S(1)}, s32[]{:S(2)}) async-start(s8[14680064]{0:T(1024)(128)(4,1)} %bitcast.70), calls=%async_computation.7 | async-start | bytes 8388608
  126.7 8.5 %slice-start.2 = ((s8[14680064]{0:T(1024)(128)(4,1)}), s8[4194304]{0:T(1024)(128)(4,1)S(1)}, s32[]{:S(2)}) async-start(s8[14680064]{0:T(1024)(128)(4,1)} %bitcast.70), calls=%async_computation.8 | async-start | bytes 8388608
  126.7 8.5 %slice-start.3 = ((s8[14680064]{0:T(1024)(128)(4,1)}), s8[2097152]{0:T(1024)(128)(4,1)S(1)}, s32[]{:S(2)}) async-start(s8[14680064]{0:T(1024)(128)(4,1)} %bitcast.70), calls=%async_computation.9 | async-start | bytes 4194304
  223.6 9.6 %copy-start = (bf16[2048,3584]{1,0:T(8,128)(2,1)S(1)}, bf16[2048,3584]{1,0:T(8,128)(2,1)}, u32[]{:S(2)}) copy-start(bf16[2048,3584]{1,0:T(8,128)(2,1)} %all-gather.8.cloned.1.call-done) | copy-start | bytes 44040196
  242.7 7.0 %copy-start.5 = (bf16[1024,512]{1,0:T(8,128)(2,1)}, bf16[1024,512]{1,0:T(8,128)(2,1)S(1)}, u32[]{:S(2)}) copy-start(bf16[1024,512]{1,0:T(8,128)(2,1)S(1)} %get-tuple-element.26) | copy-start | bytes 3145732
  242.7 29.1 %copy-start.2 = (bf16[1024,512]{1,0:T(8,128)(2,1)}, bf16[1024,512]{1,0:T(8,128)(2,1)S(1)}, u32[]{:S(2)}) copy-start(bf16[1024,512]{1,0:T(8,128)(2,1)S(1)} %get-tuple-element.25) | copy-start | bytes 3145732
  262.0 327.0 %reduce-scatter.5.cloned.1.call-start = ((), (), s32[]{:S(2)}) async-start(), calls=%async_computation.3 | async-start | bytes 15138816 | tf_op jit(solution)/shard_map/reduce_scatter | solution.py:38
  315.5 7.7 %copy-start.4 = (bf16[1024,512]{1,0:T(8,128)(2,1)S(1)}, bf16[1024,512]{1,0:T(8,128)(2,1)}, u32[]{:S(2)}) copy-start(bf16[1024,512]{1,0:T(8,128)(2,1)} %get-tuple-element.24) | copy-start | bytes 3145732
  315.5 16.4 %slice-start.4 = ((s8[14680064]{0:T(1024)(128)(4,1)}), s8[4194304]{0:T(1024)(128)(4,1)S(1)}, s32[]{:S(2)}) async-start(s8[14680064]{0:T(1024)(128)(4,1)} %bitcast.72), calls=%async_computation.10 | async-start | bytes 8388608
  315.5 16.4 %slice-start.5 = ((s8[14680064]{0:T(1024)(128)(4,1)}), s8[4194304]{0:T(1024)(128)(4,1)S(1)}, s32[]{:S(2)}) async-start(s8[14680064]{0:T(1024)(128)(4,1)} %bitcast.72), calls=%async_computation.11 | async-start | bytes 8388608
  323.2 8.8 %slice-start.6 = ((s8[14680064]{0:T(1024)(128)(4,1)}), s8[4194304]{0:T(1024)(128)(4,1)S(1)}, s32[]{:S(2)}) async-start(s8[14680064]{0:T(1024)(128)(4,1)} %bitcast.72), calls=%async_computation.12 | async-start | bytes 8388608
  323.2 8.8 %slice-start.7 = ((s8[14680064]{0:T(1024)(128)(4,1)}), s8[2097152]{0:T(1024)(128)(4,1)S(1)}, s32[]{:S(2)}) async-start(s8[14680064]{0:T(1024)(128)(4,1)} %bitcast.72), calls=%async_computation.13 | async-start | bytes 4194304
  323.2 8.8 %copy-start.3 = (bf16[1024,512]{1,0:T(8,128)(2,1)S(1)}, bf16[1024,512]{1,0:T(8,128)(2,1)}, u32[]{:S(2)}) copy-start(bf16[1024,512]{1,0:T(8,128)(2,1)} %copy-done.2) | copy-start | bytes 3145732
  390.0 8.0 %copy-start.6 = (bf16[1024,512]{1,0:T(8,128)(2,1)S(1)}, bf16[1024,512]{1,0:T(8,128)(2,1)}, u32[]{:S(2)}) copy-start(bf16[1024,512]{1,0:T(8,128)(2,1)} %copy-done.5) | copy-start | bytes 3145732
Sparse Core Ops, SparseCore 0:
  10.8 106.2 all-gather.5
  120.0 103.5 all-gather.7
  262.1 159.9 reduce-scatter.2
  424.9 164.0 reduce-scatter.4
